TPU v7x, 512 devices: a whole 4x8x8 slice. The times are simulated.
512 devices in a mesh: member: 8 (over z), lat: 16 (over x_lo, y), lon: 4 (over x_hi, core).
Axes of the slice: x: 4 (x_hi: 2, x_lo: 2; x = x_hi * 2 + x_lo), y: 8, z: 8, core: 2. Of those that a mesh axis runs over, the one named last changes fastest.
Arguments:
- inputs: bfloat16 [8, 512, 128, 512], P('member', None, 'lat', 'lon'), may hold values from -6 to 6
- weight: bfloat16 [3, 3, 100, 512], replicated, may hold values from -0.09375 to 0.09375
- bias: float32 [100], replicated, may hold values from -3 to 3
- observed: bfloat16 [100, 128, 512], P(None, 'lat', 'lon'), may hold values from -7 to 7
- channel_weight: float32 [100], replicated, may hold values from 1 to 8
Outputs:
- grad_input: bfloat16 [8, 512, 128, 512], P('member', None, 'lat', 'lon')
- grad_weight: bfloat16 [3, 3, 100, 512], replicated
- grad_bias: float32 [100], replicated
- score: bfloat16 [100, 128, 512], P(None, 'lat', 'lon')
All inputs are finite; a program needn't handle non-finite values.
Results may differ from a plain program's by a relative error of at most 0.0023.
The roundings to bfloat16 on the way count: a program that leaves them out, or rounds other values in their place, can miss the bound.
Values may be sent and summed in bfloat16 or wider, within the bound.
A program may use at most 64 MiB of HBM per device.

v0:
```python
import math

import jax
import jax.numpy as jnp
from jax import lax
from jax.sharding import PartitionSpec as P

smooth_width = 0.25


def padded_2(block, sides, width, periodic):
    for axis, dim in sides:
        count = lax.axis_size(axis)
        forward = [(i, i + 1) for i in range(count - 1)]
        if periodic:
            forward.append((count - 1, 0))
        backward = [(target, source) for source, target in forward]
        low = lax.ppermute(
            lax.slice_in_dim(block, block.shape[dim] - width, None, axis=dim), axis, forward
        )
        high = lax.ppermute(lax.slice_in_dim(block, 0, width, axis=dim), axis, backward)
        block = jnp.concatenate([low, block, high], axis=dim)
    return block


def on_device(inputs, weight, bias, observed, channel_weight):
    members = lax.axis_size("member")
    rows = inputs.shape[2]
    cols = inputs.shape[3]
    lat_rows = rows * lax.axis_size("lat")
    lon_cols = cols * lax.axis_size("lon")
    rim = padded_2(inputs, (("lat", 2),), 1, False)
    padded = padded_2(rim, (("lon", 3),), 1, True)[0]
    total = jnp.zeros((weight.shape[2], rows, cols), jnp.float32) + bias[:, None, None]
    for i in range(3):
        for j in range(3):
            total = total + jnp.einsum(
                "oc,chw->ohw",
                weight[i, j],
                padded[:, i : i + rows, j : j + cols],
                preferred_element_type=jnp.float32,
            )
    fields = total.astype(jnp.bfloat16)
    every_row = jnp.arange(lat_rows).astype(jnp.float32)
    area_mean = jnp.mean(jnp.cos(math.pi * (every_row + 0.5) / lat_rows - math.pi / 2))
    local_row = (lax.axis_index("lat") * rows + jnp.arange(rows)).astype(jnp.float32)
    area = jnp.cos(math.pi * (local_row + 0.5) / lat_rows - math.pi / 2)
    scale = channel_weight[:, None, None] * (area / area_mean)[None, :, None]
    pair_norm = members * (members - 1)
    every_member = lax.all_gather(fields[None], "member", axis=0, tiled=True)
    obs = observed.astype(jnp.float32)
    own = fields.astype(jnp.float32)
    gap_total = jnp.zeros(own.shape, jnp.float32)
    pair_total = jnp.zeros(own.shape, jnp.float32)
    for first in range(members):
        one = every_member[first].astype(jnp.float32)
        gap = one - obs
        gap_total = gap_total + jnp.sqrt(gap * gap + smooth_width * smooth_width)
        diff = one[None] - every_member.astype(jnp.float32)
        pair_total = pair_total + jnp.sum(
            jnp.sqrt(diff * diff + smooth_width * smooth_width), axis=0
        )
    own_diff = own[None] - every_member.astype(jnp.float32)
    slope = jnp.sum(own_diff / jnp.sqrt(own_diff * own_diff + smooth_width * smooth_width), axis=0)
    own_gap = own - obs
    own_root = jnp.sqrt(own_gap * own_gap + smooth_width * smooth_width)
    grad = (scale * (own_gap / own_root / members - slope / pair_norm)).astype(jnp.bfloat16)
    score = (gap_total / members - pair_total / (2 * pair_norm)).astype(jnp.bfloat16)
    grad_rim = padded_2(grad[None], (("lat", 2),), 1, False)
    grad_pad = padded_2(grad_rim, (("lon", 3),), 1, True)[0]
    back = jnp.zeros((weight.shape[3], rows, cols), jnp.float32)
    for i in range(3):
        for j in range(3):
            back = back + jnp.einsum(
                "oc,ohw->chw",
                weight[i, j],
                grad_pad[:, 2 - i : 2 - i + rows, 2 - j : 2 - j + cols],
                preferred_element_type=jnp.float32,
            )
    grad_input = back.astype(jnp.bfloat16)[None]
    pieces = []
    for i in range(3):
        for j in range(3):
            pieces.append(
                jnp.einsum(
                    "ohw,chw->oc",
                    grad,
                    padded[:, i : i + rows, j : j + cols],
                    preferred_element_type=jnp.float32,
                )
            )
    kernel = jnp.stack(pieces).reshape(3, 3, weight.shape[2], weight.shape[3])
    bias_part = jnp.sum(grad.astype(jnp.float32), axis=(1, 2))
    kernel_sum, bias_sum = lax.psum((kernel, bias_part), ("member", "lat", "lon"))
    factor = 1.0 / math.sqrt(members * lat_rows * lon_cols)
    return (grad_input, (kernel_sum * factor).astype(jnp.bfloat16), bias_sum * factor, score)


def solution(mesh):
    in_specs = (P("member", None, "lat", "lon"), P(), P(), P(None, "lat", "lon"), P())
    out_specs = (P("member", None, "lat", "lon"), P(), P(), P(None, "lat", "lon"))
    return jax.shard_map(
        on_device, mesh=mesh, in_specs=in_specs, out_specs=out_specs, check_vma=False
    )
```

profile of v0, /device:TPU:1, one launch (start us, length us, event | category | flops | bytes accessed | tf_op | source)
XLA Modules:
  0.0 511.9 jit_solution(1403849950415244985)
XLA Ops:
  7.2 2.0 fusion.177
  9.3 4.0 collective-permute-start
  13.4 1.3 collective-permute-start.1
  15.5 3.5 collective-permute-done.1
  19.1 1.6 fusion.176
  20.7 2.0 copy.34
  22.7 6.6 %collective-permute-start.2 = (bf16[1,512,10,1]{1,2,3,0:T(8,128)(2,1)S(1)}, bf16[1,512,10,1]{1,2,3,0:T(8,128)(2,1)S(1)}, u32[]{:S(2)}, u32[]{:S(2)}) collective-permute-start(bf16[1,512,10,1]{1,2,3,0:T(8,128)(2,1)S(1)} %copy.34), channel_id=1, source_target_pairs={{0,1},{1,2},{2,3},{3,0},{4,5},{5,6},{6,7},{7,4},{8,9},{9,10},{10,1... | collective-permute-start | bytes 30728 | tf_op jit(solution)/shard_map/ppermute | solution.py:18
  29.3 0.7 copy.35
  30.0 2.5 collective-permute-start.3
  33.1 3.5 collective-permute-done.3
  36.6 1.6 copy.37
  38.1 2.8 maximum_bitcast_fusion
  45.4 0.7 copy.40
  46.4 0.6 cosine_reduce_fusion
  47.9 40.6 %all-gather.3.cloned.1.call-done = bf16[800,8,128]{2,1,0:T(8,128)(2,1)} async-done(((bf16[100,8,128]{2,1,0:T(8,128)(2,1)}), bf16[800,8,128]{2,1,0:T(8,128)(2,1)}) %all-gather.3.cloned.1.call-update) | async-done | bytes 1638416 | tf_op jit(solution)/shard_map/all_gather | solution.py:50
  88.5 1.6 fusion.175
  91.1 1.1 copy-done.4
  92.2 11.6 %fusion.8 = (f32[100,8,128]{2,1,0:T(8,128)S(1)}, f32[100,8,128]{2,1,0:T(8,128)S(1)}, f32[100,8,128]{2,1,0:T(8,128)S(1)}, f32[100,8,128]{2,1,0:T(8,128)S(1)}, f32...) fusion(bf16[8,100,8,128]{3,2,1,0:T(8,128)(2,1)S(1)} %bitcast.13, ...), kind=kLoop, calls=%fused_computation.17 | loop fusion | flops 30208000 | bytes 9011200 | tf_op jit(solution)/shard_map/reduce_sum | solution.py:60
  104.5 3.1 collective-permute-start.4
  107.6 1.3 collective-permute-start.5
  112.7 1.6 fusion.120
  114.8 102.4 %psum.15 = f32[100]{0:T(128)S(1)} all-reduce(f32[100]{0:T(128)S(1)} %get-tuple-element.25), channel_id=1, replica_groups=mesh['member'=8,'lat'=16,'lon'=4] {'member','lat','lon'}, use_global_device_ids=true, to_apply=%region_4.0 | all-reduce | flops 100 | bytes 800 | tf_op jit(solution)/shard_map/psum | solution.py:94
  217.2 0.9 fusion.178
  218.1 3.2 collective-permute-start.6
  221.3 2.1 collective-permute-start.7
  224.0 0.7 copy.67
  225.0 5.9 %collective-permute-done.7 = bf16[1,100,10,1]{3,1,2,0:T(8,128)(2,1)} collective-permute-done((bf16[1,100,10,1]{3,1,2,0:T(8,128)(2,1)}, bf16[1,100,10,1]{3,1,2,0:T(8,128)(2,1)}, u32[]{:S(2)}, u32[]{:S(2)}) %collective-permute-start.7) | collective-permute-done | bytes 2032 | tf_op jit(solution)/shard_map/ppermute | solution.py:21
  230.9 1.3 maximum_bitcast_fusion.1
  236.5 0.9 fusion.37
  237.5 1.5 copy.66
  238.9 263.4 %all-reduce.2.cloned.1.call-done = f32[3,3,100,512]{3,2,1,0:T(8,128)} async-done(((f32[3,3,100,512]{3,2,1,0:T(8,128)}), f32[3,3,100,512]{3,2,1,0:T(8,128)}) %all-reduce.2.cloned.1.call-update) | async-done | bytes 1843216 | tf_op jit(solution)/shard_map/psum | solution.py:94
  502.3 2.7 multiply_convert_fusion
  (79 shorter events, 17.3 us)
Async XLA Ops:
  7.2 8.1 %copy-start.2 = (bf16[1,512,8,128]{3,2,1,0:T(8,128)(2,1)S(1)}, bf16[1,512,8,128]{3,2,1,0:T(8,128)(2,1)}, u32[]{:S(2)}) copy-start(bf16[1,512,8,128]{3,2,1,0:T(8,128)(2,1)} %param.5) | copy-start | bytes 3145732
  7.2 81.3 %all-gather.3.cloned.1.call-start = ((), (), s32[]{:S(2)}) async-start(), calls=%async_computation.1 | async-start | bytes 1843200 | tf_op jit(solution)/shard_map/all_gather | solution.py:50
  9.3 6.0 %collective-permute-start = (bf16[1,512,1,128]{3,1,2,0:T(8,128)(2,1)S(1)}, bf16[1,512,1,128]{3,1,2,0:T(8,128)(2,1)S(1)}, u32[]{:S(2)}, u32[]{:S(2)}) collective-permute-start(bf16[1,512,1,128]{3,1,2,0:T(8,128)(2,1)S(1)} %copy.150), channel_id=1, source_target_pairs={{0,4},{4,8},{8,12},{12,16},{16,20},{20,24},{24,28},{28,32},{32,36}... | collective-permute-start | bytes 393224 | tf_op jit(solution)/shard_map/ppermute | solution.py:18
  13.4 5.7 %collective-permute-start.1 = (bf16[1,512,1,128]{3,1,2,0:T(8,128)(2,1)S(1)}, bf16[1,512,1,128]{3,1,2,0:T(8,128)(2,1)S(1)}, u32[]{:S(2)}, u32[]{:S(2)}) collective-permute-start(bf16[1,512,1,128]{3,1,2,0:T(8,128)(2,1)S(1)} %copy.151), channel_id=1, source_target_pairs={{4,0},{8,4},{12,8},{16,12},{20,16},{24,20},{28,24},{32,28},{36,32}... | collective-permute-start | bytes 393224 | tf_op jit(solution)/shard_map/ppermute | solution.py:21
  22.7 9.8 %collective-permute-start.2 = (bf16[1,512,10,1]{1,2,3,0:T(8,128)(2,1)S(1)}, bf16[1,512,10,1]{1,2,3,0:T(8,128)(2,1)S(1)}, u32[]{:S(2)}, u32[]{:S(2)}) collective-permute-start(bf16[1,512,10,1]{1,2,3,0:T(8,128)(2,1)S(1)} %copy.34), channel_id=1, source_target_pairs={{0,1},{1,2},{2,3},{3,0},{4,5},{5,6},{6,7},{7,4},{8,9},{9,10},{10,1... | collective-permute-start | bytes 30728 | tf_op jit(solution)/shard_map/ppermute | solution.py:18
  30.0 6.6 %collective-permute-start.3 = (bf16[1,512,10,1]{1,2,3,0:T(8,128)(2,1)S(1)}, bf16[1,512,10,1]{1,2,3,0:T(8,128)(2,1)S(1)}, u32[]{:S(2)}, u32[]{:S(2)}) collective-permute-start(bf16[1,512,10,1]{1,2,3,0:T(8,128)(2,1)S(1)} %copy.35), channel_id=1, source_target_pairs={{1,0},{2,1},{3,2},{0,3},{5,4},{6,5},{7,6},{4,7},{9,8},{10,9},{11,1... | collective-permute-start | bytes 30728 | tf_op jit(solution)/shard_map/ppermute | solution.py:21
  38.1 2.8 copy-start.5
  41.0 4.0 copy-start
  43.6 1.5 copy-start.8
  45.0 2.7 copy-start.9
  46.2 456.1 %all-reduce.2.cloned.1.call-start = ((), (), s32[]{:S(2)}) async-start(), calls=%async_computation | async-start | bytes 3833856 | tf_op jit(solution)/shard_map/psum | solution.py:94
  90.7 1.4 copy-start.4
  92.2 11.6 %copy-start.7 = (bf16[100,8,128]{2,1,0:T(8,128)(2,1)S(1)}, bf16[100,8,128]{2,1,0:T(8,128)(2,1)}, u32[]{:S(2)}) copy-start(bf16[100,8,128]{2,1,0:T(8,128)(2,1)} %param.8) | copy-start | bytes 614404
  92.2 11.9 %copy-start.1 = (bf16[512,10,130]{2,0,1:T(8,128)(2,1)S(1)}, bf16[512,10,130]{2,0,1:T(8,128)(2,1)}, u32[]{:S(2)}) copy-start(bf16[512,10,130]{2,0,1:T(8,128)(2,1)} %copy-done) | copy-start | bytes 3993604
  104.5 112.7 %collective-permute-start.4 = (bf16[1,100,1,128]{3,1,2,0:T(8,128)(2,1)S(1)}, bf16[1,100,1,128]{3,1,2,0:T(8,128)(2,1)S(1)}, u32[]{:S(2)}, u32[]{:S(2)}) collective-permute-start(bf16[1,100,1,128]{3,1,2,0:T(8,128)(2,1)S(1)} %get-tuple-element.41), channel_id=1, source_target_pairs={{0,4},{4,8},{8,12},{12,16},{16,20},{20,24},{24,28},{28,32},{32,36}... | collective-permute-start | bytes 76808 | tf_op jit(solution)/shard_map/ppermute | solution.py:18
  107.6 109.6 %collective-permute-start.5 = (bf16[1,100,1,128]{3,1,2,0:T(8,128)(2,1)S(1)}, bf16[1,100,1,128]{3,1,2,0:T(8,128)(2,1)S(1)}, u32[]{:S(2)}, u32[]{:S(2)}) collective-permute-start(bf16[1,100,1,128]{3,1,2,0:T(8,128)(2,1)S(1)} %get-tuple-element.42), channel_id=1, source_target_pairs={{4,0},{8,4},{12,8},{16,12},{20,16},{24,20},{28,24},{32,28},{36,32}... | collective-permute-start | bytes 76808 | tf_op jit(solution)/shard_map/ppermute | solution.py:21
  114.8 109.9 %copy-start.3 = (f32[9,100,512]{2,1,0:T(8,128)}, f32[9,100,512]{2,1,0:T(8,128)S(1)}, u32[]{:S(2)}) copy-start(f32[9,100,512]{2,1,0:T(8,128)S(1)} %fusion.48) | copy-start | bytes 5529604
  218.1 14.1 %copy-start.6 = (bf16[3,3,100,512]{3,2,1,0:T(8,128)(2,1)S(1)}, bf16[3,3,100,512]{3,2,1,0:T(8,128)(2,1)}, u32[]{:S(2)}) copy-start(bf16[3,3,100,512]{3,2,1,0:T(8,128)(2,1)} %param.6) | copy-start | bytes 2764804
  218.1 6.8 %collective-permute-start.6 = (bf16[1,100,10,1]{3,1,2,0:T(8,128)(2,1)}, bf16[1,100,10,1]{3,1,2,0:T(8,128)(2,1)}, u32[]{:S(2)}, u32[]{:S(2)}) collective-permute-start(bf16[1,100,10,1]{3,1,2,0:T(8,128)(2,1)} %get-tuple-element.39), channel_id=1, source_target_pairs={{0,1},{1,2},{2,3},{3,0},{4,5},{5,6},{6,7},{7,4},{8,9},{9,10},{10,1... | collective-permute-start | bytes 6008 | tf_op jit(solution)/shard_map/ppermute | solution.py:18
  221.3 9.6 %collective-permute-start.7 = (bf16[1,100,10,1]{3,1,2,0:T(8,128)(2,1)}, bf16[1,100,10,1]{3,1,2,0:T(8,128)(2,1)}, u32[]{:S(2)}, u32[]{:S(2)}) collective-permute-start(bf16[1,100,10,1]{3,1,2,0:T(8,128)(2,1)} %get-tuple-element.40), channel_id=1, source_target_pairs={{1,0},{2,1},{3,2},{0,3},{5,4},{6,5},{7,6},{4,7},{9,8},{10,9},{11,1... | collective-permute-start | bytes 6008 | tf_op jit(solution)/shard_map/ppermute | solution.py:21
Sparse Core Ops, SparseCore 0:
  46.3 42.1 all-gather.2
  224.8 277.4 all-reduce.1
where the time goes:
time: 513 us; the launch traced here: 512 us
  waiting for transfers between devices  318 us (62%)
  blocking collectives  102 us (20%)
  starting transfers between devices  24.4 us (5%)
  other arithmetic  21.9 us (4%)
  local copies, waits for them, and re-layouts  15.9 us (3%)
  between operations  15.2 us (3%)
  matrix products  14.2 us (3%)
    psum x1, waiting for transfers between devices, on_device(): lax.psum((kernel, bias_part), ('member', 'lat', 'lon'))  263 us
    psum x1, blocking collectives, on_device(): lax.psum((kernel, bias_part), ('member', 'lat', 'lon'))  102 us
    all_gather x1, waiting for transfers between devices, on_device(): every_member = lax.all_gather(fields[None], 'member', axis=0, tiled=True)  40.6 us
    ppermute x4, starting transfers between devices, padded_2(): lax.ppermute(lax.slice_in_dim(block, block.shape[dim] - width, None, axis...  17 us
    ppermute x4, waiting for transfers between devices, padded_2(): lax.ppermute(lax.slice_in_dim(block, 0, width, axis=dim), axis, backward)  12.9 us
    reduce_sum x1, other arithmetic, on_device(): jnp.sum(jnp.sqrt(diff * diff + smooth_width * smooth_width), axis=0)  11.6 us
  transfers between devices with their start and end apart: 10, of which 7 were waited for; matrix products, arithmetic and copies ran while one was open for 3% of the time, Pallas kernels for 0%

commit v1 on v0

v1 whole, which is shorter than its diff:
```python
import functools
import math

import jax
import jax.numpy as jnp
from jax import lax
from jax.experimental import pallas as pl
from jax.experimental.pallas import tpu as pltpu
from jax.sharding import PartitionSpec as P

smooth = 0.0625
MESH = pl.DeviceIdType.MESH
F32 = jnp.float32
BF16 = jnp.bfloat16
NN = (((1,), (0,)), ((), ()))
NT = (((1,), (1,)), ((), ()))
OP = 112
OF = 104


def mm(a, b, dims=NN):
    return lax.dot_general(a, b, dims, preferred_element_type=F32)


def rcopy(src, dst, ssem, rsem, dev):
    return pltpu.make_async_remote_copy(
        src_ref=src, dst_ref=dst, send_sem=ssem, recv_sem=rsem,
        device_id=dev, device_id_type=MESH,
    )


def kernel(
    sizes,
    x_ref, w_ref, bias_ref, obs_ref, cw_ref, area_ref,
    gi_ref, gw_ref, gb_ref, score_ref,
    xf, xs, ws, wt, y, hs, hr, rows_s, rows_r, fs, fr, of, gs, gr, sc_s, sc_r,
    ce_s, ce_r, rh, gt, d4, rc, rsum, r1, s2, r2, x3, t_b, g1, g2, gif,
    sem_h, sem_row, sem_f, sem_g, sem_sc, sem_rh, sem_ce,
    sem_core, sem_1, sem_2, sem_x, sem_g1, sem_g2, sem_gc,
):
    NM, NLAT, NLON, NY, NX = sizes
    C = x_ref.shape[0]
    CO = obs_ref.shape[0]
    R = x_ref.shape[1]
    m = lax.axis_index("member")
    a = lax.axis_index("lat")
    b = lax.axis_index("lon")
    xl, yy = a // NY, a % NY
    xh, core = b // 2, b % 2
    xx = xh * 2 + xl
    up = a > 0
    down = a < NLAT - 1
    left = lax.rem(b + NLON - 1, NLON)
    right = lax.rem(b + 1, NLON)
    a_up = jnp.maximum(a - 1, 0)
    a_dn = jnp.minimum(a + 1, NLAT - 1)

    def dev_z(p):
        return (p, a, b)

    def dev_y(p):
        return (m, xl * NY + p, b)

    def dev_x(p):
        return (m, (p % 2) * NY + yy, (p // 2) * 2 + core)

    other_core = (m, a, xh * 2 + 1 - core)

    def each(n, fn):
        def body(d, carry):
            fn(d)
            return carry
        lax.fori_loop(1, n, body, 0)

    bar = pltpu.get_barrier_semaphore()

    def greet(dev):
        pl.semaphore_signal(bar, inc=1, device_id=dev, device_id_type=MESH)

    each(NM, lambda d: greet(dev_z(lax.rem(m + d, NM))))
    each(NY, lambda d: greet(dev_y(lax.rem(yy + d, NY))))
    each(NX, lambda d: greet(dev_x(lax.rem(xx + d, NX))))
    for bb in (left, right):
        greet((m, a, bb))

    @pl.when(up)
    def _():
        for bb in (b, left, right):
            greet((m, a_up, bb))

    @pl.when(down)
    def _():
        for bb in (b, left, right):
            greet((m, a_dn, bb))
    greet(other_core)

    xf[...] = x_ref[...].reshape(C * R, 128).astype(F32)
    for r in range(R):
        xs[:, r * 128:(r + 1) * 128] = xf[pl.ds(r, C, stride=R), :].astype(BF16)
    zpad = jnp.zeros((OP - CO, C), F32)
    for t in range(9):
        tap = w_ref[t // 3, t % 3].astype(F32)
        ws[t * OP:(t + 1) * OP, :] = jnp.concatenate([tap, zpad], axis=0).astype(BF16)

    cell = lax.broadcasted_iota(jnp.int32, (32, R * 128), 1)
    line = lax.broadcasted_iota(jnp.int32, (32, R * 128), 0)
    want = jnp.where(line < 16, line * 128, (line - 16) * 128 + 127)
    pick = jnp.where((cell == want) & (line % 16 < R), 1.0, 0.0).astype(BF16)
    hs[...] = mm(pick, xs[...], NT).astype(BF16).reshape(2, 16, C)

    n_hello = (NM - 1) + (NY - 1) + (NX - 1) + 3
    pl.semaphore_wait(bar, n_hello + 3 * up.astype(jnp.int32) + 3 * down.astype(jnp.int32))

    h_first = rcopy(hs.at[0], hr.at[1], sem_h.at[0], sem_h.at[3], (m, a, left))
    h_last = rcopy(hs.at[1], hr.at[0], sem_h.at[1], sem_h.at[2], (m, a, right))
    h_first.start()
    h_last.start()

    def fwd(n, carry):
        at = pl.ds(pl.multiple_of(n * 256, 256), 256)
        y[:, at] = mm(ws[...], xs[:, at])
        return carry
    lax.fori_loop(0, R // 2, fwd, 0)
    bt = jnp.broadcast_to(bias_ref[...], (128, 128)).T
    ct = jnp.broadcast_to(cw_ref[...], (128, 128)).T
    h_first.wait_recv()
    h_last.wait_recv()
    yh = mm(ws[...], hr[...].reshape(32, C), NT)

    lane = lax.broadcasted_iota(jnp.int32, (OF, 128), 1)

    def tap_rows(t):
        return slice(t * OP, t * OP + OF)

    def out_row(r):
        parts = []
        cols = []
        for j in range(3):
            total = None
            col = None
            for i in range(3):
                src = r + i - 1
                if 0 <= src < R:
                    piece = y[tap_rows(i * 3 + j), src * 128:(src + 1) * 128]
                    total = piece if total is None else total + piece
                    if j != 1:
                        at = src if j == 0 else 16 + src
                        edge = yh[tap_rows(i * 3 + j), at:at + 1]
                        col = edge if col is None else col + edge
            parts.append(total)
            cols.append(col)
        low = jnp.where(lane == 0, cols[0], pltpu.roll(parts[0], 1, 1))
        high = jnp.where(lane == 127, cols[2], pltpu.roll(parts[2], 127, 1))
        return parts[1] + low + high

    rows_s[0] = out_row(-1)
    rows_s[1] = out_row(R)
    row_up = rcopy(rows_s.at[0], rows_r.at[1], sem_row.at[0], sem_row.at[3], (m, a_up, b))
    row_dn = rcopy(rows_s.at[1], rows_r.at[0], sem_row.at[1], sem_row.at[2], (m, a_dn, b))

    @pl.when(up)
    def _():
        row_up.start()

    @pl.when(down)
    def _():
        row_dn.start()

    rows_r_zero = jnp.zeros((OF, 128), F32)
    pad8 = jnp.zeros((OP - OF, 128), F32)

    def pad16(v):
        return jnp.concatenate([v, pad8], axis=0).astype(BF16)

    for r in range(1, R - 1):
        fs[r] = pad16(out_row(r) + bt[:OF])
    first = out_row(0) + bt[:OF]
    last = out_row(R - 1) + bt[:OF]

    @pl.when(up)
    def _():
        row_dn.wait_recv()

    @pl.when(jnp.logical_not(up))
    def _():
        rows_r[0] = rows_r_zero

    @pl.when(down)
    def _():
        row_up.wait_recv()

    @pl.when(jnp.logical_not(down))
    def _():
        rows_r[1] = rows_r_zero
    fs[0] = pad16(first + rows_r[0])
    fs[R - 1] = pad16(last + rows_r[1])

    def f_copy(d):
        p = lax.rem(m + d, NM)
        return rcopy(fs.at[p], fr.at[m], sem_f.at[0, d], sem_f.at[1, d], dev_z(p))
    each(NM, lambda d: f_copy(d).start())
    fr[m] = fs[m]
    of[...] = jnp.concatenate(
        [obs_ref[...].reshape(CO * R, 128).astype(F32), jnp.zeros(((OF - CO) * R, 128), F32)], axis=0)
    obs = of[pl.ds(m, OF, stride=R), :]
    scale = ct[:OF] * area_ref[pl.ds(a * R + m, 1), :]
    each(NM, lambda d: f_copy(d).wait_recv())

    own = [fr[k][:OF].astype(F32) for k in range(NM)]
    slope = [None] * NM
    pair = jnp.full((OF, 128), NM * 0.5 * math.sqrt(smooth), F32)
    gap_total = jnp.zeros((OF, 128), F32)
    for k in range(NM):
        for n in range(k + 1, NM):
            diff = own[k] - own[n]
            sq = diff * diff + smooth
            inv = lax.rsqrt(sq)
            pair = pair + sq * inv
            s = diff * inv
            slope[k] = s if slope[k] is None else slope[k] + s
            slope[n] = -s if slope[n] is None else slope[n] - s
    for k in range(NM):
        gap = own[k] - obs
        sq = gap * gap + smooth
        inv = lax.rsqrt(sq)
        gap_total = gap_total + sq * inv
        gs[k] = pad16(scale * (gap * inv * (1.0 / NM) - slope[k] * (1.0 / (NM * (NM - 1)))))
    sc_s[...] = pad16(gap_total * (1.0 / NM) - pair * (1.0 / (NM * (NM - 1))))

    def g_copy(d):
        p = lax.rem(m + d, NM)
        return rcopy(gs.at[p], gr.at[m], sem_g.at[0, d], sem_g.at[1, d], dev_z(p))

    def sc_copy(d):
        p = lax.rem(m + d, NM)
        return rcopy(sc_s, sc_r.at[m], sem_sc.at[0, d], sem_sc.at[1, d], dev_z(p))
    each(NM, lambda d: g_copy(d).start())
    each(NM, lambda d: sc_copy(d).start())
    gr[m] = gs[m]
    sc_r[m] = sc_s[...]
    wt[:, :9 * OP] = ws[...].astype(F32).T.astype(BF16)
    wt[:, 9 * OP:] = jnp.zeros((C, 1024 - 9 * OP), BF16)
    each(NM, lambda d: g_copy(d).wait_recv())

    g_up = rcopy(gr.at[0], rh.at[1], sem_rh.at[0], sem_rh.at[3], (m, a_up, b))
    g_dn = rcopy(gr.at[R - 1], rh.at[0], sem_rh.at[1], sem_rh.at[2], (m, a_dn, b))

    @pl.when(up)
    def _():
        g_up.start()

    @pl.when(down)
    def _():
        g_dn.start()
    edges = []
    lane8 = lax.broadcasted_iota(jnp.int32, (8, 128), 1)
    line8 = lax.broadcasted_iota(jnp.int32, (8, 128), 0)
    pick2 = jnp.where(((line8 == 0) & (lane8 == 0)) | ((line8 == 1) & (lane8 == 127)), 1.0, 0.0).astype(BF16)
    for r in range(R):
        edges.append(mm(pick2, gr[r], NT))
    fill = jnp.zeros((16 - R, OP), F32)
    for side in range(2):
        stack = jnp.concatenate([e[side:side + 1] for e in edges] + [fill], axis=0)
        ce_s[side] = jnp.concatenate([stack, jnp.zeros((16, 128 - OP), F32)], axis=1).astype(BF16)

    def c_copy(v, s):
        aa = (a_dn, a, a_up)[v]
        bb = right if s == 0 else left
        return rcopy(ce_s.at[1 - s], ce_r.at[v, s], sem_ce.at[0, v, s], sem_ce.at[1, v, s], (m, aa, bb))

    for s in range(2):
        c_copy(1, s).start()

    @pl.when(down)
    def _():
        for s in range(2):
            c_copy(0, s).start()

    @pl.when(up)
    def _():
        for s in range(2):
            c_copy(2, s).start()

    for s in range(2):
        c_copy(1, s).wait_recv()

    @pl.when(up)
    def _():
        g_dn.wait_recv()
        for s in range(2):
            c_copy(0, s).wait_recv()

    @pl.when(jnp.logical_not(up))
    def _():
        rh[0] = jnp.zeros((OP, 128), BF16)
        for s in range(2):
            ce_r[0, s] = jnp.zeros((16, 128), BF16)

    @pl.when(down)
    def _():
        g_up.wait_recv()
        for s in range(2):
            c_copy(2, s).wait_recv()

    @pl.when(jnp.logical_not(down))
    def _():
        rh[1] = jnp.zeros((OP, 128), BF16)
        for s in range(2):
            ce_r[2, s] = jnp.zeros((16, 128), BF16)

    colt = []
    for s in range(2):
        above = ce_r[0, s].astype(F32)[R - 1:R]
        here = ce_r[1, s].astype(F32)[:R]
        below = ce_r[2, s].astype(F32)[0:1]
        stack = jnp.concatenate([above, here, below, jnp.zeros((128 - R - 2, 128), F32)], axis=0)
        colt.append(stack.T)
    lane_p = lax.broadcasted_iota(jnp.int32, (OP, 128), 1)
    for q in range(R + 2):
        r = q - 1
        mid = rh[0] if r < 0 else rh[1] if r >= R else gr[r]
        wide = mid.astype(F32)
        to_right = jnp.where(lane_p == 127, colt[1][:OP, q:q + 1], pltpu.roll(wide, 127, 1)).astype(BF16)
        to_left = jnp.where(lane_p == 0, colt[0][:OP, q:q + 1], pltpu.roll(wide, 1, 1)).astype(BF16)
        for i in range(3):
            here = r - 1 + i
            if 0 <= here < R:
                for j, v in enumerate((to_right, mid, to_left)):
                    t = i * 3 + j
                    gt[t * OP:(t + 1) * OP, here * 128:(here + 1) * 128] = v
    gt[9 * OP:, :] = jnp.zeros((1024 - 9 * OP, R * 128), BF16)

    half = C // 2

    def wgrad(h):
        at = pl.ds(pl.multiple_of(h * half, half), half)
        part = mm(gt[:9 * OP, :], xs[at, :], NT)
        for q in range(2):
            d4[h * 2 + q, :9 * OP, :] = part[:, q * 128:(q + 1) * 128]

    center = mm(jnp.ones((16, R * 128), BF16), gt[4 * OP:5 * OP, :], NT)
    bias_rows = jnp.concatenate([center, jnp.zeros((16, 128 - OP), F32)], axis=1)
    for q in range(4):
        d4[q, 9 * OP:, :] = bias_rows if q == 0 else jnp.zeros((16, 128), F32)
    wgrad(1 - core)
    core_copy = rcopy(d4.at[pl.ds(2 * (1 - core), 2)], rc, sem_core.at[0], sem_core.at[1], other_core)
    core_copy.start()
    wgrad(core)
    core_copy.wait_recv()
    rsum[...] = d4[pl.ds(2 * core, 2)] + rc[...]

    n1 = (NY, NM)
    me1 = (yy, m)
    dev1 = (dev_y, dev_z)
    n2 = (NM, NY)
    me2 = (m, yy)
    dev2 = (dev_z, dev_y)

    def copy1(q, d):
        p = lax.rem(me1[q] + d, n1[q])
        return rcopy(rsum.at[q, pl.ds(pl.multiple_of(p * 128, 128), 128)], r1.at[q, d],
                     sem_1.at[0, q, d], sem_1.at[1, q, d], dev1[q](p))

    def start1(d):
        for q in range(2):
            copy1(q, d).start()
    each(NY, start1)

    def bwd(n, carry):
        at = pl.ds(pl.multiple_of(n * 256, 256), 256)
        part = mm(wt[...], gt[:, at])
        for q in range(2):
            gif[pl.ds(2 * n + q, C, stride=R), :] = part[:, q * 128:(q + 1) * 128]
        return carry
    lax.fori_loop(0, R // 2, bwd, 0)
    gi_ref[...] = gif[...].reshape(C, R, 128).astype(BF16)
    each(NM, lambda d: sc_copy(d).wait_recv())
    for r in range(R):
        of[pl.ds(r, OF, stride=R), :] = sc_r[r].astype(F32)[:OF]
    score_ref[...] = of[:CO * R, :].reshape(CO, R, 128).astype(BF16)

    for q in range(2):
        total = rsum[q, pl.ds(pl.multiple_of(me1[q] * 128, 128), 128), :]
        for d in range(1, n1[q]):
            copy1(q, d).wait_recv()
            total = total + r1[q, d]
        s2[q] = total

    def copy2(q, d):
        p = lax.rem(me2[q] + d, n2[q])
        return rcopy(s2.at[q, pl.ds(pl.multiple_of(p * 16, 16), 16)], r2.at[q, d],
                     sem_2.at[0, q, d], sem_2.at[1, q, d], dev2[q](p))

    def start2(d):
        for q in range(2):
            copy2(q, d).start()
    each(NY, start2)
    for q in range(2):
        total = s2[q, pl.ds(pl.multiple_of(me2[q] * 16, 16), 16), :]
        for d in range(1, n2[q]):
            copy2(q, d).wait_recv()
            total = total + r2[q, d]
        x3[xx, q] = total

    def copy3(d):
        p = lax.rem(xx + d, NX)
        return rcopy(x3.at[xx], x3.at[xx], sem_x.at[0, d], sem_x.at[1, d], dev_x(p))
    each(NX, lambda d: copy3(d).start())
    each(NX, lambda d: copy3(d).wait_recv())
    factor = 1.0 / math.sqrt(NM * NLAT * R * NLON * 128)
    sub = lax.broadcasted_iota(jnp.int32, (16, 128), 0)
    for q in range(2):
        total = x3[0, q]
        for p in range(1, NX):
            total = total + x3[p, q]
        total = total * factor
        high = total.astype(BF16).astype(F32)
        rest = total - high
        middle = rest.astype(BF16).astype(F32)
        low = rest - middle
        row = me1[q] * 128 + me2[q] * 16 + sub
        t_b[q] = jnp.where(row == 9 * OP + 1, middle, jnp.where(row == 9 * OP + 2, low, high)).astype(BF16)

    def copy_g1(q, d):
        p = lax.rem(me2[q] + d, n2[q])
        return rcopy(t_b.at[q], g1.at[q, me2[q]], sem_g1.at[0, q, d], sem_g1.at[1, q, d], dev2[q](p))

    def start_g1(d):
        for q in range(2):
            copy_g1(q, d).start()
    each(NY, start_g1)
    for q in range(2):
        g1[q, me2[q]] = t_b[q]

    def wait_g1(d):
        for q in range(2):
            copy_g1(q, d).wait_recv()
    each(NY, wait_g1)

    def copy_g2(q, d):
        p = lax.rem(me1[q] + d, n1[q])
        return rcopy(g1.at[q], g2.at[core * 2 + q, me1[q]], sem_g2.at[0, q, d], sem_g2.at[1, q, d], dev1[q](p))

    def start_g2(d):
        for q in range(2):
            copy_g2(q, d).start()
    each(NY, start_g2)
    for q in range(2):
        g2[core * 2 + q, me1[q]] = g1[q]

    def wait_g2(d):
        for q in range(2):
            copy_g2(q, d).wait_recv()
    each(NY, wait_g2)
    mine = g2.at[pl.ds(2 * core, 2)]
    last_copy = rcopy(mine, mine, sem_gc.at[0], sem_gc.at[1], other_core)
    last_copy.start()
    last_copy.wait_recv()

    for q in range(4):
        flat = g2[q].reshape(1024, 128)
        for t in range(9):
            gw_ref[t // 3, t % 3, :, q * 128:(q + 1) * 128] = flat[t * OP:t * OP + CO]
        if q == 0:
            tail = flat[9 * OP:9 * OP + 16].astype(F32)
            gb_ref[...] = (tail[0:1] + tail[1:2] + tail[2:3])[:, :CO]

    h_first.wait_send()
    h_last.wait_send()

    @pl.when(up)
    def _():
        row_up.wait_send()
        g_up.wait_send()
        for s in range(2):
            c_copy(2, s).wait_send()

    @pl.when(down)
    def _():
        row_dn.wait_send()
        g_dn.wait_send()
        for s in range(2):
            c_copy(0, s).wait_send()
    for s in range(2):
        c_copy(1, s).wait_send()

    def finish(d):
        f_copy(d).wait_send()
        g_copy(d).wait_send()
        sc_copy(d).wait_send()
        for q in range(2):
            copy1(q, d).wait_send()
            copy2(q, d).wait_send()
            copy_g1(q, d).wait_send()
            copy_g2(q, d).wait_send()
    each(NM, finish)
    each(NX, lambda d: copy3(d).wait_send())
    core_copy.wait_send()
    last_copy.wait_send()


def solution(mesh):
    NM, NLAT, NLON = (mesh.shape[k] for k in ("member", "lat", "lon"))
    NY, NX = NLAT // 2, NLON // 2 * 2
    sizes = (NM, NLAT, NLON, NY, NX)

    def on_device(inputs, weight, bias, observed, channel_weight):
        _, C, R, L = inputs.shape
        CO = weight.shape[2]
        rows = NLAT * R
        mean = 1.0 / (rows * math.sin(math.pi / (2 * rows)))
        every = jnp.asarray([math.sin(math.pi * (r + 0.5) / rows) / mean for r in range(rows)], F32)
        area = jnp.broadcast_to(every[:, None], (rows, 128))
        pad = ((0, 0), (0, 128 - CO))
        vm = pl.BlockSpec(memory_space=pltpu.VMEM)
        dma = pltpu.SemaphoreType.DMA
        V = pltpu.VMEM
        scratch = [
            V((C * R, 128), F32),
            V((C, R * 128), BF16),
            V((9 * OP, C), BF16),
            V((C, 1024), BF16),
            V((9 * OP, R * 128), F32),
            V((2, 16, C), BF16),
            V((2, 16, C), BF16),
            V((2, OF, 128), F32),
            V((2, OF, 128), F32),
            V((R, OP, 128), BF16),
            V((NM, OP, 128), BF16),
            V((OF * R, 128), F32),
            V((NM, OP, 128), BF16),
            V((R, OP, 128), BF16),
            V((OP, 128), BF16),
            V((R, OP, 128), BF16),
            V((2, 16, 128), BF16),
            V((3, 2, 16, 128), BF16),
            V((2, OP, 128), BF16),
            V((1024, R * 128), BF16),
            V((4, 1024, 128), F32),
            V((2, 1024, 128), F32),
            V((2, 1024, 128), F32),
            V((2, NY, 128, 128), F32),
            V((2, 128, 128), F32),
            V((2, NY, 16, 128), F32),
            V((NX, 2, 16, 128), F32),
            V((2, 16, 128), BF16),
            V((2, NY, 16, 128), BF16),
            V((4, NY, NY, 16, 128), BF16),
            V((C * R, 128), F32),
            dma((4,)), dma((4,)), dma((2, NM)), dma((2, NM)), dma((2, NM)), dma((4,)), dma((2, 3, 2)),
            dma((2,)), dma((2, 2, NY)), dma((2, 2, NY)), dma((2, NX)), dma((2, 2, NY)), dma((2, 2, NY)), dma((2,)),
        ]
        gi, gw, gb, score = pl.pallas_call(
            functools.partial(kernel, sizes),
            out_shape=(
                jax.ShapeDtypeStruct((C, R, L), BF16),
                jax.ShapeDtypeStruct((3, 3, CO, C), BF16),
                jax.ShapeDtypeStruct((1, CO), F32),
                jax.ShapeDtypeStruct((CO, R, L), BF16),
            ),
            in_specs=[vm] * 6,
            out_specs=(vm,) * 4,
            scratch_shapes=scratch,
            compiler_params=pltpu.CompilerParams(
                collective_id=0, has_side_effects=True, vmem_limit_bytes=56 * 1024 * 1024),
        )(inputs[0], weight, jnp.pad(bias[None], pad), observed, jnp.pad(channel_weight[None], pad), area)
        return gi[None], gw, gb[0], score

    in_specs = (P("member", None, "lat", "lon"), P(), P(), P(None, "lat", "lon"), P())
    out_specs = (P("member", None, "lat", "lon"), P(), P(), P(None, "lat", "lon"))
    return jax.shard_map(
        on_device, mesh=mesh, in_specs=in_specs, out_specs=out_specs, check_vma=False
    )
```

time: 513 us -> 99.2 us (0.19)
  waiting for transfers between devices: 318 us -> 0 us
  blocking collectives: 102 us -> 0 us
  Pallas kernels: 0 us -> 91.2 us
  starting transfers between devices: 24.4 us -> 0 us
  other arithmetic: 21.9 us -> 0 us
  between operations: 15.2 us -> 0.66 us
  matrix products: 14.2 us -> 0 us
  local copies, waits for them, and re-layouts: 15.9 us -> 7.16 us
    psum x1 -> x0, waiting for transfers between devices: 263 us -> none  [on_device(): lax.psum((kernel, bias_part), ('member', 'lat', 'lon'))]
    psum x1 -> x0, blocking collectives: 102 us -> none  [on_device(): lax.psum((kernel, bias_part), ('member', 'lat', 'lon'))]
    pallas_call x0 -> x1, Pallas kernels: none -> 91.2 us  [on_device(): pl.pallas_call(functools.partial(kernel, sizes), out_shape=(jax.ShapeDtyp...]
    all_gather x1 -> x0, waiting for transfers between devices: 40.6 us -> none  [on_device(): every_member = lax.all_gather(fields[None], 'member', axis=0, tiled=True)]
    ppermute x8 -> x0, starting transfers between devices: 24.2 us -> none  [the longest x4 17 us: padded_2(): lax.ppermute(lax.slice_in_dim(block, block.shape[dim] - width, None, axis...]
    dot_general x27 -> x0, matrix products: 14.2 us -> none  [the longest x9 5.19 us: on_device(): jnp.einsum('oc,ohw->chw', weight[i, j], grad_pad[:, 2 - i:2 - i + rows, 2...]
    ppermute x8 -> x0, waiting for transfers between devices: 13.8 us -> none  [the longest x4 12.9 us: padded_2(): lax.ppermute(lax.slice_in_dim(block, 0, width, axis=dim), axis, backward)]
    reduce_sum x3 -> x0, other arithmetic: 12.5 us -> none  [the longest x1 11.6 us: on_device(): jnp.sum(jnp.sqrt(diff * diff + smooth_width * smooth_width), axis=0)]
  transfers between devices with their start and end apart: 10 -> 0, of which waited for: 7 -> 0; matrix products, arithmetic and copies ran while one was open for 3% -> 0% of each run, Pallas kernels for 0% -> 0%
where the time goes in v1:
time: 99.2 us; the launch traced here: 99 us
  Pallas kernels  91.2 us (92%)
  local copies, waits for them, and re-layouts  7.16 us (7%)
    pallas_call x1, Pallas kernels, on_device(): pl.pallas_call(functools.partial(kernel, sizes), out_shape=(jax.ShapeDtyp...  91.2 us
    unnamed x16, local copies, waits for them, and re-layouts  5.42 us

profile of v1, /device:TPU:1, one launch (start us, length us, event | category | flops | bytes accessed | tf_op | source)
XLA Modules:
  0.0 99.0 jit_solution(12676484311474895291)
XLA Ops:
  0.6 0.0 copy-start.3
  0.6 0.6 copy-done.3
  1.3 0.0 copy-start.4
  1.3 0.5 pad.7.bias_ref
  1.8 0.1 copy-done.4
  1.9 0.0 copy-start.2
  1.9 0.5 pad.8.cw_ref
  2.5 0.1 copy-done.2
  2.6 0.7 broadcast_in_dim.17.area_ref
  3.3 91.2 %shard_map.93 = (bf16[512,8,128]{2,1,0:T(8,128)(2,1)}, bf16[3,3,100,512]{3,2,1,0:T(8,128)(2,1)}, f32[1,100]{1,0:T(1,128)}, bf16[100,8,128]{2,1,0:T(8,128)(2,1)}) custom-call(bf16[512,8,128]{2,1,0:T(8,128)(2,1)} %bitcast.5, bf16[3,3,100,512]{3,2,1,0:T(8,128)(2,1)} %w_ref.1, f32[1,128]{1,0:T(1,128)} %pad.7.bias_ref, bf16[100,8,128]{2,1,0:T(8,128)(2,1)} %obs_ref.1, ...), custom_call_target="tpu_custom_call" | custom-call | tf_op jit(solution)/shard_map/pallas_call | solution.py:553
  94.5 0.0 copy-start
  94.5 2.3 %copy.14 = bf16[1,512,8,128]{3,2,1,0:T(8,128)(2,1)} copy(bf16[1,512,8,128]{3,2,1,0:T(8,128)(2,1)} %bitcast.6) | data formatting | bytes 2097152
  96.9 0.0 copy-done
  96.9 0.0 copy-start.5
  96.9 0.0 copy-start.1
  96.9 0.9 copy.15
  97.8 0.0 copy-done.5
  97.8 0.5 copy.16
  98.3 0.0 copy-done.1
  98.3 0.7 copy.17
Async XLA Ops:
  0.6 0.7 copy-start.3
  1.3 0.7 copy-start.4
  1.9 0.7 copy-start.2
  94.5 2.4 %copy-start = (bf16[3,3,100,512]{3,2,1,0:T(8,128)(2,1)S(1)}, bf16[3,3,100,512]{3,2,1,0:T(8,128)(2,1)}, u32[]{:S(2)}) copy-start(bf16[3,3,100,512]{3,2,1,0:T(8,128)(2,1)} %get-tuple-element.17) | copy-start | bytes 2764804
  96.9 0.9 copy-start.5
  96.9 1.5 %copy-start.1 = (bf16[100,8,128]{2,1,0:T(8,128)(2,1)S(1)}, bf16[100,8,128]{2,1,0:T(8,128)(2,1)}, u32[]{:S(2)}) copy-start(bf16[100,8,128]{2,1,0:T(8,128)(2,1)} %get-tuple-element.19) | copy-start | bytes 614404

commit v2 on v1

v2 whole, which is shorter than its diff:
```python
import functools
import math

import jax
import jax.numpy as jnp
from jax import lax
from jax.experimental import pallas as pl
from jax.experimental.pallas import tpu as pltpu
from jax.sharding import PartitionSpec as P

smooth = 0.0625
MESH = pl.DeviceIdType.MESH
F32 = jnp.float32
BF16 = jnp.bfloat16
NN = (((1,), (0,)), ((), ()))
NT = (((1,), (1,)), ((), ()))
OP = 112
OF = 104


def mm(a, b, dims=NN):
    return lax.dot_general(a, b, dims, preferred_element_type=F32)


def rcopy(src, dst, ssem, rsem, dev):
    return pltpu.make_async_remote_copy(
        src_ref=src, dst_ref=dst, send_sem=ssem, recv_sem=rsem,
        device_id=dev, device_id_type=MESH,
    )


def kernel(
    sizes,
    x_in, w_in, bias_in, obs_in, cw_in,
    gi_ref, gw_ref, gb_ref, score_ref,
    x_ref, w_ref, bias_ref, obs_ref, cw_ref, sem_in,
    xf, xs, ws, wt, y, acc, yh, hs, hr, rows_s, rows_r, scale_s, fs, fr, of, gs, gr, sc_s, sc_r,
    ce_s, ce_r, rh, gt, d4, rc, rsum, r1, s3, t_b, g2, gif,
    sem_h, sem_row, sem_f, sem_g, sem_sc, sem_rh, sem_ce,
    sem_core, sem_1, sem_2, sem_g1, sem_gc, sem_here,
):
    NM, NLAT, NLON, NY, NX = sizes
    C = x_in.shape[0]
    CO = obs_in.shape[0]
    R = x_in.shape[1]
    m = lax.axis_index("member")
    a = lax.axis_index("lat")
    b = lax.axis_index("lon")
    xl, yy = a // NY, a % NY
    xh, core = b // 2, b % 2
    xx = xh * 2 + xl
    up = a > 0
    down = a < NLAT - 1
    left = lax.rem(b + NLON - 1, NLON)
    right = lax.rem(b + 1, NLON)
    a_up = jnp.maximum(a - 1, 0)
    a_dn = jnp.minimum(a + 1, NLAT - 1)

    def dev_z(p):
        return (p, a, b)

    def dev_y(p):
        return (m, xl * NY + p, b)

    def dev_x(p):
        return (m, (p % 2) * NY + yy, (p // 2) * 2 + core)

    other_core = (m, a, xh * 2 + 1 - core)

    def each(n, fn):
        def body(d, carry):
            fn(d)
            return carry
        lax.fori_loop(1, n, body, 0)

    pairs = ((x_in, x_ref), (w_in, w_ref), (bias_in, bias_ref), (cw_in, cw_ref), (obs_in, obs_ref))
    loads = [pltpu.make_async_copy(src, dst, sem_in.at[i]) for i, (src, dst) in enumerate(pairs)]
    for load in loads:
        load.start()
    sends = []
    late = []

    bar = pltpu.get_barrier_semaphore()

    def greet(dev):
        pl.semaphore_signal(bar, inc=1, device_id=dev, device_id_type=MESH)

    def peer(g, e, back=False):
        sign = -1 if back else 1
        p = (xx + NX + sign * (e // 8)) % NX
        step = NY + sign * (e % 8)
        y2 = (yy + step) % NY if g == 0 else yy
        m2 = (m + step) % NM if g == 1 else m
        return p, y2, m2

    def dev_of(p, y2, m2):
        return (m2, (p % 2) * NY + y2, (p // 2) * 2 + core)

    each(NM, lambda d: greet(dev_z(lax.rem(m + d, NM))))
    each(NY, lambda d: greet(dev_y(lax.rem(yy + d, NY))))
    each(NX, lambda d: greet(dev_x(lax.rem(xx + d, NX))))
    for bb in (left, right):
        greet((m, a, bb))

    @pl.when(up)
    def _():
        for bb in (b, left, right):
            greet((m, a_up, bb))

    @pl.when(down)
    def _():
        for bb in (b, left, right):
            greet((m, a_dn, bb))
    greet(other_core)

    loads[0].wait()
    xf[...] = x_ref[...].reshape(C * R, 128).astype(F32)
    for r in range(R):
        xs[:, r * 128:(r + 1) * 128] = xf[pl.ds(r, C, stride=R), :].astype(BF16)
    cell = lax.broadcasted_iota(jnp.int32, (32, R * 128), 1)
    line = lax.broadcasted_iota(jnp.int32, (32, R * 128), 0)
    want = jnp.where(line < 16, line * 128, (line - 16) * 128 + 127)
    pick = jnp.where((cell == want) & (line % 16 < R), 1.0, 0.0).astype(BF16)
    hs[...] = mm(pick, xs[...], NT).astype(BF16).reshape(2, 16, C)

    for load in loads[1:]:
        load.wait()
    zpad = jnp.zeros((OP - CO, C), F32)
    for t in range(9):
        tap = w_ref[t // 3, t % 3].astype(F32)
        ws[t * OP:(t + 1) * OP, :] = jnp.concatenate([tap, zpad], axis=0).astype(BF16)


    lane = lax.broadcasted_iota(jnp.int32, (OF, 128), 1)

    def shifted(p0, p1, p2):
        low = jnp.where(lane == 0, 0.0, pltpu.roll(p0, 1, 1))
        high = jnp.where(lane == 127, 0.0, pltpu.roll(p2, 127, 1))
        return p1 + low + high

    rows_s[0] = shifted(*[mm(ws[(6 + j) * OP:(6 + j) * OP + OF, :], xs[:, :128]) for j in range(3)])
    rows_s[1] = shifted(*[mm(ws[j * OP:j * OP + OF, :], xs[:, (R - 1) * 128:]) for j in range(3)])
    n_hello = (NM - 1) + (NY - 1) + (NX - 1) + 3
    pl.semaphore_wait(bar, n_hello + 3 * up.astype(jnp.int32) + 3 * down.astype(jnp.int32))
    each(NX, lambda d: pl.semaphore_signal(
        sem_here, inc=1, device_id=dev_x(lax.rem(xx + d, NX)), device_id_type=MESH))

    x_up = rcopy(rows_s.at[0], rows_r.at[1], sem_row.at[0], sem_row.at[3], (m, a_up, b))
    x_dn = rcopy(rows_s.at[1], rows_r.at[0], sem_row.at[1], sem_row.at[2], (m, a_dn, b))

    def h_copy(v, s):
        aa = (a_dn, a, a_up)[v]
        bb = right if s == 0 else left
        return rcopy(hs.at[1 - s], hr.at[v, s], sem_h.at[0, v, s], sem_h.at[1, v, s], (m, aa, bb))

    def both(fn):
        for s in range(2):
            fn(s)

    both(lambda s: h_copy(1, s).start())

    @pl.when(up)
    def _():
        both(lambda s: h_copy(2, s).start())
        x_up.start()

    @pl.when(down)
    def _():
        both(lambda s: h_copy(0, s).start())
        x_dn.start()

    def x_sent():
        both(lambda s: h_copy(1, s).wait_send())

        @pl.when(up)
        def _():
            x_up.wait_send()
            both(lambda s: h_copy(2, s).wait_send())

        @pl.when(down)
        def _():
            x_dn.wait_send()
            both(lambda s: h_copy(0, s).wait_send())
    sends.append(x_sent)

    for n in range(R // 2):
        at = slice(n * 256, (n + 1) * 256)
        y[:, at] = mm(ws[...], xs[:, at])
    fill = jnp.zeros((1, 128 - CO), F32)
    bt = jnp.broadcast_to(jnp.concatenate([bias_ref[...], fill], axis=1), (128, 128)).T
    ct = jnp.broadcast_to(jnp.concatenate([cw_ref[...], fill], axis=1), (128, 128)).T
    rows = NLAT * R
    row_at = jnp.full((8, 128), (a * R + m).astype(F32))
    area = jnp.cos(math.pi * (row_at + 0.5) / rows - math.pi / 2)
    area_mean = 1.0 / (rows * math.sin(math.pi / (2 * rows)))
    scale_s[...] = ct[:OP] * (area * (1.0 / area_mean))[0:1]

    def tap_rows(t):
        return slice(t * OP, t * OP + OF)

    for r in range(R):
        parts = []
        for j in range(3):
            total = None
            for i in range(3):
                src = r + i - 1
                if 0 <= src < R:
                    piece = y[tap_rows(i * 3 + j), src * 128:(src + 1) * 128]
                    total = piece if total is None else total + piece
            parts.append(total)
        acc[r] = shifted(*parts) + bt[:OF]

    both(lambda s: h_copy(1, s).wait_recv())

    @pl.when(up)
    def _():
        both(lambda s: h_copy(0, s).wait_recv())

    @pl.when(jnp.logical_not(up))
    def _():
        hr[0] = jnp.zeros((2, 16, C), BF16)

    @pl.when(down)
    def _():
        both(lambda s: h_copy(2, s).wait_recv())

    @pl.when(jnp.logical_not(down))
    def _():
        hr[2] = jnp.zeros((2, 16, C), BF16)
    yh[...] = mm(ws[...], hr[...].reshape(96, C), NT)

    pad8 = jnp.zeros((OP - OF, 128), F32)

    def pad16(v):
        return jnp.concatenate([v, pad8], axis=0).astype(BF16)

    def columns(r):
        cols = []
        for j in (0, 2):
            col = None
            for i in range(3):
                src = r + i - 1
                at = 8 * j + (R - 1 if src < 0 else 64 if src >= R else 32 + src)
                edge = yh[tap_rows(i * 3 + j), at:at + 1]
                col = edge if col is None else col + edge
            cols.append(col)
        return jnp.where(lane == 0, cols[0], jnp.where(lane == 127, cols[1], 0.0))

    def f_copy(d):
        p = lax.rem(m + d, NM)
        return rcopy(fs.at[p], fr.at[m], sem_f.at[0, d], sem_f.at[1, d], dev_z(p))

    def make_row(r):
        total = acc[r] + columns(r)
        if r == 0:
            total = total + rows_r[0]
        if r == R - 1:
            total = total + rows_r[1]
        fs[r] = pad16(total)

        @pl.when(m != r)
        def _():
            f_copy(lax.rem(r - m + NM, NM)).start()

    for r in range(1, R - 1):
        make_row(r)

    @pl.when(up)
    def _():
        x_dn.wait_recv()

    @pl.when(jnp.logical_not(up))
    def _():
        rows_r[0] = jnp.zeros((OF, 128), F32)

    @pl.when(down)
    def _():
        x_up.wait_recv()

    @pl.when(jnp.logical_not(down))
    def _():
        rows_r[1] = jnp.zeros((OF, 128), F32)
    make_row(0)
    make_row(R - 1)
    fr[m] = fs[m]
    sends.append(lambda: each(NM, lambda d: f_copy(d).wait_send()))
    of[...] = jnp.concatenate(
        [obs_ref[...].reshape(CO * R, 128).astype(F32), jnp.zeros(((OP - CO) * R, 128), F32)], axis=0)
    wt[:, :9 * OP] = ws[...].T
    wt[:, 9 * OP:] = jnp.zeros((C, 1024 - 9 * OP), BF16)
    each(NM, lambda d: f_copy(d).wait_recv())

    def score(c, carry):
        at = pl.ds(pl.multiple_of(c * 16, 16), 16)
        obs = of[pl.ds(c * (16 * R) + m, 16, stride=R), :]
        own = [fr[k, at, :].astype(F32) for k in range(NM)]
        slope = [None] * NM
        pair = jnp.full((16, 128), NM * 0.5 * math.sqrt(smooth), F32)
        gap_total = jnp.zeros((16, 128), F32)
        for k in range(NM):
            for n in range(k + 1, NM):
                diff = own[k] - own[n]
                sq = diff * diff + smooth
                inv = lax.rsqrt(sq)
                pair = pair + sq * inv
                s = diff * inv
                slope[k] = s if slope[k] is None else slope[k] + s
                slope[n] = -s if slope[n] is None else slope[n] - s
        for k in range(NM):
            gap = own[k] - obs
            sq = gap * gap + smooth
            inv = lax.rsqrt(sq)
            gap_total = gap_total + sq * inv
            gs[k, at, :] = (scale_s[at, :] * (
                gap * inv * (1.0 / NM) - slope[k] * (1.0 / (NM * (NM - 1))))).astype(BF16)
        sc_s[at, :] = (gap_total * (1.0 / NM) - pair * (1.0 / (NM * (NM - 1)))).astype(BF16)
        return carry
    lax.fori_loop(0, OP // 16, score, 0)

    def g_copy(d):
        p = lax.rem(m + d, NM)
        return rcopy(gs.at[p], gr.at[m], sem_g.at[0, d], sem_g.at[1, d], dev_z(p))

    def sc_copy(d):
        p = lax.rem(m + d, NM)
        return rcopy(sc_s, sc_r.at[m], sem_sc.at[0, d], sem_sc.at[1, d], dev_z(p))
    each(NM, lambda d: g_copy(d).start())
    gr[m] = gs[m]
    sends.append(lambda: each(NM, lambda d: g_copy(d).wait_send()))
    sc_r[m] = sc_s[...]
    each(NM, lambda d: g_copy(d).wait_recv())

    g_up = rcopy(gr.at[0], rh.at[1], sem_rh.at[0], sem_rh.at[3], (m, a_up, b))
    g_dn = rcopy(gr.at[R - 1], rh.at[0], sem_rh.at[1], sem_rh.at[2], (m, a_dn, b))

    @pl.when(up)
    def _():
        g_up.start()

    @pl.when(down)
    def _():
        g_dn.start()
    edges = []
    lane8 = lax.broadcasted_iota(jnp.int32, (8, 128), 1)
    line8 = lax.broadcasted_iota(jnp.int32, (8, 128), 0)
    pick2 = jnp.where(((line8 == 0) & (lane8 == 0)) | ((line8 == 1) & (lane8 == 127)), 1.0, 0.0).astype(BF16)
    for r in range(R):
        edges.append(mm(pick2, gr[r], NT))
    fill = jnp.zeros((16 - R, OP), F32)
    for side in range(2):
        stack = jnp.concatenate([e[side:side + 1] for e in edges] + [fill], axis=0)
        ce_s[side] = jnp.concatenate([stack, jnp.zeros((16, 128 - OP), F32)], axis=1).astype(BF16)

    def c_copy(v, s):
        aa = (a_dn, a, a_up)[v]
        bb = right if s == 0 else left
        return rcopy(ce_s.at[1 - s], ce_r.at[v, s], sem_ce.at[0, v, s], sem_ce.at[1, v, s], (m, aa, bb))

    for s in range(2):
        c_copy(1, s).start()

    @pl.when(down)
    def _():
        for s in range(2):
            c_copy(0, s).start()

    @pl.when(up)
    def _():
        for s in range(2):
            c_copy(2, s).start()

    def edges_sent():
        for s in range(2):
            c_copy(1, s).wait_send()

        @pl.when(up)
        def _():
            g_up.wait_send()
            for s in range(2):
                c_copy(2, s).wait_send()

        @pl.when(down)
        def _():
            g_dn.wait_send()
            for s in range(2):
                c_copy(0, s).wait_send()
    sends.append(edges_sent)

    for s in range(2):
        c_copy(1, s).wait_recv()

    @pl.when(up)
    def _():
        g_dn.wait_recv()
        for s in range(2):
            c_copy(0, s).wait_recv()

    @pl.when(jnp.logical_not(up))
    def _():
        rh[0] = jnp.zeros((OP, 128), BF16)
        for s in range(2):
            ce_r[0, s] = jnp.zeros((16, 128), BF16)

    @pl.when(down)
    def _():
        g_up.wait_recv()
        for s in range(2):
            c_copy(2, s).wait_recv()

    @pl.when(jnp.logical_not(down))
    def _():
        rh[1] = jnp.zeros((OP, 128), BF16)
        for s in range(2):
            ce_r[2, s] = jnp.zeros((16, 128), BF16)

    colt = []
    for s in range(2):
        above = ce_r[0, s].astype(F32)[R - 1:R]
        here = ce_r[1, s].astype(F32)[:R]
        below = ce_r[2, s].astype(F32)[0:1]
        stack = jnp.concatenate([above, here, below, jnp.zeros((128 - R - 2, 128), F32)], axis=0)
        colt.append(stack.T)
    lane_p = lax.broadcasted_iota(jnp.int32, (OP, 128), 1)
    for q in range(R + 2):
        r = q - 1
        mid = rh[0] if r < 0 else rh[1] if r >= R else gr[r]
        wide = mid.astype(F32)
        to_right = jnp.where(lane_p == 127, colt[1][:OP, q:q + 1], pltpu.roll(wide, 127, 1)).astype(BF16)
        to_left = jnp.where(lane_p == 0, colt[0][:OP, q:q + 1], pltpu.roll(wide, 1, 1)).astype(BF16)
        for i in range(3):
            here = r - 1 + i
            if 0 <= here < R:
                for j, v in enumerate((to_right, mid, to_left)):
                    t = i * 3 + j
                    gt[t * OP:(t + 1) * OP, here * 128:(here + 1) * 128] = v
    gt[9 * OP:, :] = jnp.zeros((1024 - 9 * OP, R * 128), BF16)

    half = C // 2

    def wgrad(h):
        at = pl.ds(pl.multiple_of(h * half, half), half)
        part = mm(gt[:9 * OP, :], xs[at, :], NT)
        for q in range(2):
            d4[h * 2 + q, :9 * OP, :] = part[:, q * 128:(q + 1) * 128]

    center = mm(jnp.ones((16, R * 128), BF16), gt[4 * OP:5 * OP, :], NT)
    bias_rows = jnp.concatenate([center, jnp.zeros((16, 128 - OP), F32)], axis=1)
    for q in range(4):
        d4[q, 9 * OP:, :] = bias_rows if q == 0 else jnp.zeros((16, 128), F32)
    wgrad(1 - core)
    core_copy = rcopy(d4.at[pl.ds(2 * (1 - core), 2)], rc, sem_core.at[0], sem_core.at[1], other_core)
    core_copy.start()
    sends.append(core_copy.wait_send)
    wgrad(core)
    core_copy.wait_recv()
    rsum[...] = d4[pl.ds(2 * core, 2)] + rc[...]

    own_chunk = (xx * NY + yy, xx * NM + m)

    def copy1(q, e):
        p, y2, m2 = peer(q, e)
        at = (p * 8 + (m2 if q else y2)) * 32
        return rcopy(rsum.at[q, pl.ds(pl.multiple_of(at, 32), 32)], r1.at[q, e],
                     sem_1.at[0, q, e], sem_1.at[1, q, e], dev_of(p, y2, m2))

    pl.semaphore_wait(sem_here, NX - 1)

    def start1(e):
        for q in range(2):
            copy1(q, e).start()
    each(32, start1)
    sends.append(lambda: each(32, lambda e: [copy1(q, e).wait_send() for q in range(2)]))
    each(NM, lambda d: sc_copy(d).start())
    sends.append(lambda: each(NM, lambda d: sc_copy(d).wait_send()))
    late.append(lambda: each(NM, lambda d: sc_copy(d).wait_recv()))

    def bwd(n, carry):
        at = pl.ds(pl.multiple_of(n * 256, 256), 256)
        part = mm(wt[...], gt[:, at])
        for q in range(2):
            gif[pl.ds(2 * n + q, C, stride=R), :] = part[:, q * 128:(q + 1) * 128]
        return carry
    lax.fori_loop(0, R // 2, bwd, 0)
    gi_ref[...] = gif[...].reshape(C, R, 128).astype(BF16)
    me2 = (m, yy)
    for q in range(2):
        def add(e, total):
            copy1(q, e).wait_recv()
            return total + r1[q, e]
        s3[q, me2[q]] = lax.fori_loop(
            1, 32, add, rsum[q, pl.ds(pl.multiple_of(own_chunk[q] * 32, 32), 32), :])

    def copy2(q, d):
        p = lax.rem(me2[q] + d, 8)
        mine = s3.at[q, me2[q]]
        return rcopy(mine, mine, sem_2.at[0, q, d], sem_2.at[1, q, d], dev_y(p) if q else dev_z(p))

    def start2(d):
        for q in range(2):
            copy2(q, d).start()
    each(8, start2)
    sends.append(lambda: each(8, lambda d: [copy2(q, d).wait_send() for q in range(2)]))

    def wait2(d):
        for q in range(2):
            copy2(q, d).wait_recv()
    each(8, wait2)
    factor = 1.0 / math.sqrt(NM * NLAT * R * NLON * 128)
    sub = lax.broadcasted_iota(jnp.int32, (32, 128), 0)
    for q in range(2):
        total = s3[q, 0]
        for p in range(1, 8):
            total = total + s3[q, p]
        total = total * factor
        high = total.astype(BF16).astype(F32)
        rest = total - high
        middle = rest.astype(BF16).astype(F32)
        low = rest - middle
        row = own_chunk[q] * 32 + sub
        t_b[q] = jnp.where(row == 9 * OP + 1, middle, jnp.where(row == 9 * OP + 2, low, high)).astype(BF16)

    def copy_g(q, e):
        return rcopy(t_b.at[q], g2.at[core * 2 + q, own_chunk[q]], sem_g1.at[0, q, e], sem_g1.at[1, q, e],
                     dev_of(*peer(q, e)))

    def start_g(e):
        for q in range(2):
            copy_g(q, e).start()
    each(32, start_g)
    sends.append(lambda: each(32, lambda e: [copy_g(q, e).wait_send() for q in range(2)]))
    for q in range(2):
        g2[core * 2 + q, own_chunk[q]] = t_b[q]

    def copy_c(q, k):
        at = pl.ds(pl.multiple_of(((xx + NX - k) % NX) * 8, 8), 8)
        block = g2.at[core * 2 + q, at]
        return rcopy(block, block, sem_gc.at[0, q, k], sem_gc.at[1, q, k], other_core)

    def pass_on(k, carry):
        def got(d, inner):
            for q in range(2):
                @pl.when(k + d > 0)
                def _():
                    copy_g(q, k * 8 + d).wait_recv()
            return inner
        lax.fori_loop(0, 8, got, 0)
        for q in range(2):
            copy_c(q, k).start()
        return carry
    lax.fori_loop(0, NX, pass_on, 0)

    def each_c(fn):
        def body(k, carry):
            for q in range(2):
                fn(copy_c(q, k))
            return carry
        lax.fori_loop(0, NX, body, 0)
    sends.append(lambda: each_c(lambda c: c.wait_send()))
    late.pop()()
    for r in range(R):
        of[pl.ds(r, OF, stride=R), :] = sc_r[r].astype(F32)[:OF]
    score_ref[...] = of[:CO * R, :].reshape(CO, R, 128).astype(BF16)

    each_c(lambda c: c.wait_recv())

    for q in range(4):
        flat = g2[q].reshape(1024, 128)
        for t in range(9):
            gw_ref[t // 3, t % 3, :, q * 128:(q + 1) * 128] = flat[t * OP:t * OP + CO]
        if q == 0:
            tail = flat[9 * OP:9 * OP + 16].astype(F32)
            gb_ref[...] = (tail[0:1] + tail[1:2] + tail[2:3])[:, :CO]

    for done in late + sends:
        done()


def write_out(*refs):
    loads, stores = [], []
    for k, cuts in enumerate((4, 3, 1, 1)):
        size = refs[k].shape[0] // cuts
        for c in range(cuts):
            at = pl.ds(c * size, size)
            n = len(loads)
            loads.append(pltpu.make_async_copy(refs[k].at[at], refs[8 + k].at[at], refs[12].at[0, n]))
            stores.append(pltpu.make_async_copy(refs[8 + k].at[at], refs[4 + k].at[at], refs[12].at[1, n]))
    for load in loads:
        load.start()
    for load, store in zip(loads, stores):
        load.wait()
        store.start()
    for store in stores:
        store.wait()


def solution(mesh):
    NM, NLAT, NLON = (mesh.shape[k] for k in ("member", "lat", "lon"))
    NY, NX = NLAT // 2, NLON // 2 * 2
    sizes = (NM, NLAT, NLON, NY, NX)

    def on_device(inputs, weight, bias, observed, channel_weight):
        _, C, R, L = inputs.shape
        CO = weight.shape[2]
        vm = pl.BlockSpec(memory_space=pltpu.VMEM)
        hbm = pl.BlockSpec(memory_space=pltpu.HBM)
        dma = pltpu.SemaphoreType.DMA
        V = pltpu.VMEM
        scratch = [
            V((C, R, 128), BF16), V((3, 3, CO, C), BF16), V((1, CO), F32), V((CO, R, 128), BF16), V((1, CO), F32), dma((5,)),
            V((C * R, 128), F32),
            V((C, R * 128), BF16),
            V((9 * OP, C), BF16),
            V((C, 1024), BF16),
            V((9 * OP, R * 128), F32),
            V((R, OF, 128), F32),
            V((9 * OP, 96), F32),
            V((2, 16, C), BF16),
            V((3, 2, 16, C), BF16),
            V((2, OF, 128), F32),
            V((2, OF, 128), F32),
            V((OP, 128), F32),
            V((R, OP, 128), BF16),
            V((NM, OP, 128), BF16),
            V((OP * R, 128), F32),
            V((NM, OP, 128), BF16),
            V((R, OP, 128), BF16),
            V((OP, 128), BF16),
            V((R, OP, 128), BF16),
            V((2, 16, 128), BF16),
            V((3, 2, 16, 128), BF16),
            V((2, OP, 128), BF16),
            V((1024, R * 128), BF16),
            V((4, 1024, 128), F32),
            V((2, 1024, 128), F32),
            V((2, 1024, 128), F32),
            V((2, 32, 32, 128), F32),
            V((2, 8, 32, 128), F32),
            V((2, 32, 128), BF16),
            V((4, 32, 32, 128), BF16),
            V((C * R, 128), F32),
            dma((2, 3, 2)), dma((4,)), dma((2, NM)), dma((2, NM)), dma((2, NM)), dma((4,)), dma((2, 3, 2)),
            dma((2,)), dma((2, 2, 32)), dma((2, 2, 8)), dma((2, 2, 32)), dma((2, 2, NX)),
            pltpu.SemaphoreType.REGULAR,
        ]
        shapes = (
            jax.ShapeDtypeStruct((C, R, L), BF16),
            jax.ShapeDtypeStruct((3, 3, CO, C), BF16),
            jax.ShapeDtypeStruct((1, CO), F32),
            jax.ShapeDtypeStruct((CO, R, L), BF16),
        )
        results = pl.pallas_call(
            functools.partial(kernel, sizes),
            out_shape=shapes,
            in_specs=[hbm] * 5,
            out_specs=(vm,) * 4,
            scratch_shapes=scratch,
            compiler_params=pltpu.CompilerParams(
                collective_id=0, has_side_effects=True, vmem_limit_bytes=58 * 1024 * 1024),
        )(inputs[0], weight, bias[None], observed, channel_weight[None])
        gi, gw, gb, score = pl.pallas_call(
            write_out,
            out_shape=shapes,
            in_specs=[hbm] * 4,
            out_specs=(hbm,) * 4,
            scratch_shapes=[V(shape.shape, shape.dtype) for shape in shapes] + [dma((2, 9))],
            compiler_params=pltpu.CompilerParams(vmem_limit_bytes=58 * 1024 * 1024),
        )(*results)
        return gi[None], gw, gb[0], score

    in_specs = (P("member", None, "lat", "lon"), P(), P(), P(None, "lat", "lon"), P())
    out_specs = (P("member", None, "lat", "lon"), P(), P(), P(None, "lat", "lon"))
    return jax.shard_map(
        on_device, mesh=mesh, in_specs=in_specs, out_specs=out_specs, check_vma=False
    )
```

time: 99.2 us -> 88.2 us (0.89)
  local copies, waits for them, and re-layouts: 7.16 us -> 0 us
  Pallas kernels: 91.2 us -> 87.4 us
    unnamed x16 -> x0, local copies, waits for them, and re-layouts: 5.42 us -> none
    pallas_call x1 -> x2, Pallas kernels: 91.2 us -> 87.4 us  [the longest x1 84.9 us: on_device(): pl.pallas_call(functools.partial(kernel, sizes), out_shape=shapes, in_spe...]
    pad x2 -> x0, local copies, waits for them, and re-layouts: 1.03 us -> none  [the longest x1 0.51 us: on_device(): jnp.pad(channel_weight[None], pad)]
where the time goes in v2:
time: 88.2 us; the launch traced here: 88 us
  Pallas kernels  87.4 us (99%)
    pallas_call x1, Pallas kernels, on_device(): pl.pallas_call(functools.partial(kernel, sizes), out_shape=shapes, in_spe...  84.9 us
    pallas_call x1, Pallas kernels, on_device(): pl.pallas_call(write_out, out_shape=shapes, in_specs=[hbm] * 4, out_specs...  2.45 us

profile of v2, /device:TPU:1, one launch (start us, length us, event | category | flops | bytes accessed | tf_op | source)
XLA Modules:
  0.0 88.0 jit_solution(6127008476279951158)
XLA Ops:
  0.6 84.9 %shard_map.84 = (bf16[512,8,128]{2,1,0:T(8,128)(2,1)}, bf16[3,3,100,512]{3,2,1,0:T(8,128)(2,1)}, f32[1,100]{1,0:T(1,128)}, bf16[100,8,128]{2,1,0:T(8,128)(2,1)}) custom-call(bf16[512,8,128]{2,1,0:T(8,128)(2,1)} %bitcast.5, bf16[3,3,100,512]{3,2,1,0:T(8,128)(2,1)} %w_in.1, f32[1,100]{1,0:T(1,128)} %bitcast.6, bf16[100,8,128]{2,1,0:T(8,128)(2,1)} %obs_in.1, ...), custom_call_target="tpu_custom_call" | custom-call | tf_op jit(solution)/shard_map/pallas_call | solution.py:651
  85.6 2.5 %shard_map.85 = (bf16[512,8,128]{2,1,0:T(8,128)(2,1)}, bf16[3,3,100,512]{3,2,1,0:T(8,128)(2,1)}, f32[1,100]{1,0:T(1,128)}, bf16[100,8,128]{2,1,0:T(8,128)(2,1)}) custom-call(bf16[512,8,128]{2,1,0:T(8,128)(2,1)} %get-tuple-element.12.refs_0_, bf16[3,3,100,512]{3,2,1,0:T(8,128)(2,1)} %get-tuple-element.13.refs_1_, f32[1,100]{1,0:T(1,128)} %get-tuple-element.14.refs_2_, ...), custom_call_target="tpu_custom_call" | custom-call | tf_op jit(solution)/shard_map/pallas_call | solution.py:660

commit v3 on v2

--- a/solution.py
+++ b/solution.py
@@ -227,7 +227,16 @@
     @pl.when(jnp.logical_not(down))
     def _():
         hr[2] = jnp.zeros((2, 16, C), BF16)
-    yh[...] = mm(ws[...], hr[...].reshape(96, C), NT)
+    lines = []
+    for s in range(2):
+        lines += [hr[0, s].astype(F32)[R - 1:R], hr[1, s].astype(F32)[:R], hr[2, s].astype(F32)[0:1],
+                  jnp.zeros((14 - R, C), F32)]
+    lines.append(jnp.zeros((96, C), F32))
+    yh[...] = mm(ws[...], jnp.concatenate(lines, axis=0).astype(BF16), NT)
+    sides = []
+    for j in (0, 2):
+        sides.append(yh[tap_rows(j), :] + pltpu.roll(yh[tap_rows(3 + j), :], 127, 1)
+                     + pltpu.roll(yh[tap_rows(6 + j), :], 126, 1))
 
     pad8 = jnp.zeros((OP - OF, 128), F32)
 
@@ -235,16 +244,9 @@
         return jnp.concatenate([v, pad8], axis=0).astype(BF16)
 
     def columns(r):
-        cols = []
-        for j in (0, 2):
-            col = None
-            for i in range(3):
-                src = r + i - 1
-                at = 8 * j + (R - 1 if src < 0 else 64 if src >= R else 32 + src)
-                edge = yh[tap_rows(i * 3 + j), at:at + 1]
-                col = edge if col is None else col + edge
-            cols.append(col)
-        return jnp.where(lane == 0, cols[0], jnp.where(lane == 127, cols[1], 0.0))
+        low = sides[0][:, r:r + 1]
+        high = sides[1][:, 16 + r:17 + r]
+        return jnp.where(lane == 0, low, jnp.where(lane == 127, high, 0.0))
 
     def f_copy(d):
         p = lax.rem(m + d, NM)
@@ -577,7 +579,7 @@
 
 def write_out(*refs):
     loads, stores = [], []
-    for k, cuts in enumerate((4, 3, 1, 1)):
+    for k, cuts in enumerate((8, 3, 1, 2)):
         size = refs[k].shape[0] // cuts
         for c in range(cuts):
             at = pl.ds(c * size, size)
@@ -613,7 +615,7 @@
             V((C, 1024), BF16),
             V((9 * OP, R * 128), F32),
             V((R, OF, 128), F32),
-            V((9 * OP, 96), F32),
+            V((9 * OP, 128), F32),
             V((2, 16, C), BF16),
             V((3, 2, 16, C), BF16),
             V((2, OF, 128), F32),
@@ -662,7 +664,7 @@
             out_shape=shapes,
             in_specs=[hbm] * 4,
             out_specs=(hbm,) * 4,
-            scratch_shapes=[V(shape.shape, shape.dtype) for shape in shapes] + [dma((2, 9))],
+            scratch_shapes=[V(shape.shape, shape.dtype) for shape in shapes] + [dma((2, 14))],
             compiler_params=pltpu.CompilerParams(vmem_limit_bytes=58 * 1024 * 1024),
         )(*results)
         return gi[None], gw, gb[0], score

time: 88.2 us -> 88 us (level)
  no operation moved by 1% of the time
where the time goes in v3:
time: 88 us; the launch traced here: 87.9 us
  Pallas kernels  87.2 us (99%)
    pallas_call x1, Pallas kernels, on_device(): pl.pallas_call(functools.partial(kernel, sizes), out_shape=shapes, in_spe...  84.6 us
    pallas_call x1, Pallas kernels, on_device(): pl.pallas_call(write_out, out_shape=shapes, in_specs=[hbm] * 4, out_specs...  2.63 us

profile of v3, /device:TPU:1, one launch (start us, length us, event | category | flops | bytes accessed | tf_op | source)
XLA Modules:
  0.0 87.9 jit_solution(10944923896488440708)
XLA Ops:
  0.6 84.6 %shard_map.84 = (bf16[512,8,128]{2,1,0:T(8,128)(2,1)}, bf16[3,3,100,512]{3,2,1,0:T(8,128)(2,1)}, f32[1,100]{1,0:T(1,128)}, bf16[100,8,128]{2,1,0:T(8,128)(2,1)}) custom-call(bf16[512,8,128]{2,1,0:T(8,128)(2,1)} %bitcast.5, bf16[3,3,100,512]{3,2,1,0:T(8,128)(2,1)} %w_in.1, f32[1,100]{1,0:T(1,128)} %bitcast.6, bf16[100,8,128]{2,1,0:T(8,128)(2,1)} %obs_in.1, ...), custom_call_target="tpu_custom_call" | custom-call | tf_op jit(solution)/shard_map/pallas_call | solution.py:653
  85.2 2.6 %shard_map.85 = (bf16[512,8,128]{2,1,0:T(8,128)(2,1)}, bf16[3,3,100,512]{3,2,1,0:T(8,128)(2,1)}, f32[1,100]{1,0:T(1,128)}, bf16[100,8,128]{2,1,0:T(8,128)(2,1)}) custom-call(bf16[512,8,128]{2,1,0:T(8,128)(2,1)} %get-tuple-element.12.refs_0_, bf16[3,3,100,512]{3,2,1,0:T(8,128)(2,1)} %get-tuple-element.13.refs_1_, f32[1,100]{1,0:T(1,128)} %get-tuple-element.14.refs_2_, ...), custom_call_target="tpu_custom_call" | custom-call | tf_op jit(solution)/shard_map/pallas_call | solution.py:662
